TPU v7x, 32 devices: a whole 2x2x4 slice. The times are simulated.
32 devices in a mesh: front: 4 (over z), row: 4 (over x, core), col: 2 (over y).
Axes of the slice: x: 2, y: 2, z: 4, core: 2. Of those that a mesh axis runs over, the one named last changes fastest.
Arguments:
- front_orig: float32 [4, 8192, 8192], P('front', 'row', 'col'), may hold values from -6 to 6
- children: float32 [4, 2048, 2048], P('front', 'row', 'col'), may hold values from -6 to 6
- parent_of: int32 [4], P('front'), may hold values from 0 to 3, as said below
- child_map: int32 [4, 8], P('front'), may hold values from 0 to 31, as said below
- block_mask: int32 [4, 32, 32], P('front'), may hold values 0 or 1
- pivot: int32 [4, 32], P('front'), may hold values from 0 to 31, each once within a row
- diag_inverse: float32 [4, 2, 512, 512], P('front'), may hold values from -0.01171875 to 0.01171875
Outputs:
- factored: float32 [4, 8192, 8192], P('front', 'row', 'col')
Inputs may be any that keep to these rules, and one draw needn't show every extreme that they name: `parent_of`: each front is the parent of exactly one child update. Each row of child_map is strictly increasing.
All inputs are finite; a program needn't handle non-finite values. No bound on the sum of `block_mask` on one device may be relied on, other than what follows from the above.
Results may differ from a plain program's by a relative error of at most 0.00011.
Values sent between devices are 32-bit elements; how exact they have to be, the bound alone decides.
A program may use at most 256 MiB of HBM per device.

v0:
```python
import jax
import jax.numpy as jnp
from jax import lax
from jax.sharding import PartitionSpec as P

BS = 256


HIGH = lax.Precision.HIGHEST


def from_root(x, axis, root):
    mine = lax.axis_index(axis) == root
    return lax.psum(jnp.where(mine, x, jnp.zeros_like(x)), axis)


def body(front_orig, children, parent_of, child_map, block_mask, pivot, diag_inverse):
    row_count = lax.axis_size("row")
    col_count = lax.axis_size("col")
    row_id = lax.axis_index("row")
    col_id = lax.axis_index("col")
    front_id = lax.axis_index("front")
    matrix_in = front_orig[0]
    loc_rows, loc_cols = matrix_in.shape
    row_blocks = loc_rows // BS
    col_blocks = loc_cols // BS
    kid_count = children.shape[0]
    kid_rows = children.shape[1] // BS
    kid_cols = children.shape[2] // BS

    def spread(grid):
        return jnp.broadcast_to(grid[:, None, :, None], (row_blocks, BS, col_blocks, BS)).reshape(
            loc_rows, loc_cols
        )

    all_kids, all_parents, all_maps = (
        lax.all_gather(children, "front", axis=0, tiled=True),
        lax.all_gather(parent_of, "front", axis=0, tiled=True),
        lax.all_gather(child_map, "front", axis=0, tiled=True),
    )
    child_count = all_parents.shape[0]
    serial = jnp.arange(child_count, dtype=jnp.int32)
    sort_keys = jnp.where(all_parents == front_id, serial, serial + child_count)
    owned_ids = jnp.argsort(sort_keys)[:kid_count]
    own_pieces = jnp.take(all_kids, owned_ids, axis=0)
    own_maps = jnp.take(all_maps, owned_ids, axis=0)
    child_blocks = own_maps.shape[1]
    block_ranks = jnp.arange(child_blocks, dtype=jnp.int32)

    def locate(first, width):
        target = first + jnp.arange(width, dtype=jnp.int32)
        matches = own_maps[:, :, None] == target[None, None, :]
        source = jnp.sum(jnp.where(matches, block_ranks[None, :, None], 0), axis=1)
        return (source, jnp.any(matches, axis=1).astype(jnp.float32))

    row_src, row_has = locate(row_id * row_blocks, row_blocks)
    col_src, col_has = locate(col_id * col_blocks, col_blocks)
    gathered = lax.all_gather(own_pieces[None], ("row", "col"), axis=0, tiled=True)
    child_tiles = gathered.reshape(row_count, col_count, kid_count, kid_rows, BS, kid_cols, BS)
    kid_ids = jnp.arange(kid_count, dtype=jnp.int32)
    picked = child_tiles[
        (row_src // kid_rows)[:, :, None],
        (col_src // kid_cols)[:, None, :],
        kid_ids[:, None, None],
        (row_src % kid_rows)[:, :, None],
        :,
        (col_src % kid_cols)[:, None, :],
        :,
    ]
    picked = picked * (row_has[:, :, None] * col_has[:, None, :])[:, :, :, None, None]
    extended = jnp.sum(picked, axis=0).transpose(0, 2, 1, 3).reshape(loc_rows, loc_cols)
    mask_local = lax.dynamic_slice(
        block_mask[0], (row_id * row_blocks, col_id * col_blocks), (row_blocks, col_blocks)
    ).astype(jnp.float32)
    matrix = spread(mask_local) * (matrix_in + extended)
    order = pivot[0]
    nblocks = order.shape[0]
    ranks = jnp.arange(nblocks, dtype=jnp.int32)
    position = jnp.sum(jnp.where(order[:, None] == ranks[None, :], ranks[:, None], 0), axis=0)
    for step in range(diag_inverse.shape[1]):
        alive = (position >= 2 * step + 2).astype(jnp.float32)
        alive_rows = lax.dynamic_slice_in_dim(alive, row_id * row_blocks, row_blocks)
        alive_cols = lax.dynamic_slice_in_dim(alive, col_id * col_blocks, col_blocks)
        row_live = jnp.repeat(alive_rows, BS)
        inverse = diag_inverse[0, step]
        col_parts = []
        row_parts = []
        col_owners = []
        col_slots = []
        for half in range(2):
            chosen = order[2 * step + half]
            owner_col = chosen // col_blocks
            slot_col = chosen % col_blocks
            piece = lax.dynamic_slice_in_dim(matrix, slot_col * BS, BS, 1)
            col_parts.append(from_root(piece, "col", owner_col))
            strip = lax.dynamic_slice_in_dim(matrix, chosen % row_blocks * BS, BS, 0)
            row_parts.append(from_root(strip, "row", chosen // row_blocks))
            col_owners.append(owner_col)
            col_slots.append(slot_col)
        column_panel = jnp.concatenate(col_parts, axis=1)
        row_panel = jnp.concatenate(row_parts, axis=0)
        lower = jnp.dot(column_panel, inverse, precision=HIGH, preferred_element_type=jnp.float32)
        update = jnp.dot(
            lower * row_live[:, None], row_panel, precision=HIGH, preferred_element_type=jnp.float32
        )
        lower_parts = [lower[:, :BS], lower[:, BS:]]
        live_mask = spread(mask_local * alive_rows[:, None] * alive_cols[None, :])
        fresh = matrix - update * live_mask
        for half in range(2):
            current = lax.dynamic_slice_in_dim(fresh, col_slots[half] * BS, BS, 1)
            written = jnp.where(row_live[:, None] > 0, lower_parts[half], current)
            replaced = lax.dynamic_update_slice_in_dim(fresh, written, col_slots[half] * BS, 1)
            fresh = jnp.where(col_id == col_owners[half], replaced, fresh)
        matrix = fresh
    return matrix[None]


def solution(mesh):
    placed = (
        P("front", "row", "col"),
        P("front", "row", "col"),
        P("front"),
        P("front", None),
        P("front", None, None),
        P("front", None),
        P("front", None, None, None),
    )
    return jax.shard_map(
        body, mesh=mesh, in_specs=placed, out_specs=P("front", "row", "col"), check_vma=False
    )
```

profile of v0, /device:TPU:0, one launch (start us, length us, event | category | flops | bytes accessed | tf_op | source)
XLA Modules:
  0.0 1136.1 jit_solution(10430206397553176984)
XLA Ops:
  6.5 0.7 all-gather.5.cloned.1.call-update
  8.0 1.2 dynamic-slice.17
  9.2 0.8 dynamic-update-slice.7
  10.0 9.9 all-reduce
  19.9 0.7 sort.17
  20.7 140.6 %all-gather.5.cloned.1.call-done = f32[4,512,1024]{2,1,0:T(8,128)} async-done(((f32[1,512,1024]{2,1,0:T(8,128)}), f32[4,512,1024]{2,1,0:T(8,128)}) %all-gather.5.cloned.1.call-update) | async-done | bytes 8388624 | tf_op jit(solution)/shard_map/all_gather | solution.py:37
  161.3 3.2 dynamic-slice_select_fusion.4
  164.5 0.0 all-reduce.16.cloned.1.call-start
  164.6 7.8 all-gather.1
  172.4 0.7 fusion.47
  178.4 0.1 fusion.30
  178.4 0.1 fusion.31
  178.6 0.1 constant_dynamic-update-slice_fusion.4
  178.6 0.1 constant_dynamic-update-slice_fusion.1
  178.7 0.1 reshape.643
  178.8 0.1 compare_reduce_fusion.1
  178.9 0.1 compare_reduce_fusion
  179.0 0.1 select_reduce_fusion
  179.1 0.5 compare_convert_fusion.1
  179.6 0.1 dynamic_slice.62
  179.7 0.1 dynamic_slice.65
  179.8 1.3 multiply_multiply_fusion
  181.1 4.8 broadcast_in_dim.145
  185.9 36.3 %copy.15 = f32[256,8,16,256]{3,1,2,0:T(8,128)} copy(f32[256,8,16,256]{3,2,1,0:T(8,128)S(1)} %bitcast.61) | data formatting | bytes 67108864
  222.2 0.1 broadcast_multiply_fusion
  222.3 30.5 %all-gather.7.cloned.1.call-done = f32[8,512,1024]{2,1,0:T(8,128)} async-done(((f32[1,512,1024]{2,1,0:T(8,128)}), f32[8,512,1024]{2,1,0:T(8,128)}) %all-gather.7.cloned.1.call-update) | async-done | bytes 16777232 | tf_op jit(solution)/shard_map/all_gather | solution.py:58
  252.8 20.4 %reshape.590 = f32[4,2,1,2,256,4,256]{6,5,4,3,1,0,2:T(4,128)} reshape(f32[8,512,1024]{2,1,0:T(8,128)} %all-gather.7.cloned.1.call-done) | data formatting | bytes 33554432 | tf_op jit(solution)/shard_map/reshape | solution.py:59
  273.2 14.1 %copy.13 = f32[4,2,1,2,256,4,256]{6,4,5,3,2,1,0:T(8,128)} copy(f32[4,2,1,2,256,4,256]{6,5,4,3,1,0,2:T(4,128)} %reshape.590) | data formatting | bytes 33554432 | tf_op jit(solution)/shard_map/reshape | solution.py:59
  287.2 19.5 %gather_fusion = f32[128,256,256]{2,1,0:T(8,128)} fusion(f32[4,2,1,2,256,4,256]{6,4,5,3,2,1,0:T(8,128)} %copy.13, s32[128]{0:T(128)S(1)} %reshape.643), kind=kCustom, calls=%fused_computation | custom fusion | bytes 67111424 | tf_op jit(solution)/shard_map/gather | solution.py:61
  306.8 13.1 %multiply_bitcast_fusion = f32[8,256,16,256]{3,1,2,0:T(8,128)S(1)} fusion(f32[8,16,256,256]{3,2,1,0:T(8,128)} %bitcast.57, f32[8,16]{1,0:T(8,128)S(1)} %broadcast_multiply_fusion), kind=kLoop, calls=%fused_computation.5 | loop fusion | flops 8388608 | bytes 67109376 | tf_op jit(solution)/shard_map/transpose | solution.py:71
  319.9 21.5 %copy.14 = f32[8,256,16,256]{3,2,1,0:T(8,128)} copy(f32[8,256,16,256]{3,1,2,0:T(8,128)S(1)} %multiply_bitcast_fusion) | data formatting | bytes 67108864 | tf_op jit(solution)/shard_map/transpose | solution.py:71
  341.4 38.1 %copy.16 = f32[256,8,16,256]{3,1,2,0:T(8,128)} copy(f32[256,8,16,256]{3,2,1,0:T(8,128)} %bitcast.58) | data formatting | bytes 67108864
  379.5 43.8 %fusion = f32[2048,4096]{1,0:T(8,128)} fusion(f32[2048,4096]{1,0:T(8,128)} %bitcast.62, f32[2048,4096]{1,0:T(8,128)} %bitcast.63, f32[1,2048,4096]{2,1,0:T(8,128)} %param.7), kind=kLoop, calls=%fused_computation.2 | loop fusion | flops 16777216 | bytes 134217728 | tf_op jit(solution)/shard_map/mul | solution.py:75
  423.3 4.6 dynamic-slice_select_fusion.8
  427.9 0.0 all-reduce.12.cloned.1.call-start
  428.1 8.0 dynamic-slice_select_fusion.3
  436.1 0.0 all-reduce.14.cloned.1.call-start
  436.1 0.5 copy-done.10
  436.6 0.1 dynamic_slice.54
  436.7 0.1 dynamic_slice.57
  441.9 0.1 multiply_multiply_fusion.1
  441.9 5.2 broadcast_in_dim.162
  447.2 36.2 %copy.18 = f32[256,8,16,256]{3,1,2,0:T(8,128)} copy(f32[256,8,16,256]{3,2,1,0:T(8,128)S(1)} %bitcast.59) | data formatting | bytes 67108864
  483.4 0.1 broadcast_bitcast_fusion.1
  483.5 53.6 %all-reduce.16.cloned.1.call-done = (f32[2048,256]{1,0:T(8,128)}, f32[2048,256]{1,0:T(8,128)}) async-done(((f32[2048,256]{1,0:T(8,128)}, f32[2048,256]{1,0:T(8,128)}), (f32[2048,256]{1,0:T(8,128)}, f32[2048,256]{1,0:T(8,128)})) %all-reduce.16.cloned.1.call-update) | async-done | bytes 4194320 | tf_op jit(solution)/shard_map/psum | solution.py:14
  537.1 9.8 fusion.7
  546.9 146.0 %all-reduce.12.cloned.1.call-done = (f32[256,4096]{1,0:T(8,128)}, f32[256,4096]{1,0:T(8,128)}) async-done(((f32[256,4096]{1,0:T(8,128)}, f32[256,4096]{1,0:T(8,128)}), (f32[256,4096]{1,0:T(8,128)}, f32[256,4096]{1,0:T(8,128)})) %all-reduce.12.cloned.1.call-update) | async-done | bytes 8388624 | tf_op jit(solution)/shard_map/psum | solution.py:14
  692.9 66.5 %multiply_subtract_fusion.1 = f32[2048,4096]{1,0:T(8,128)} fusion(f32[2048,4096]{1,0:T(8,128)} %fusion, f32[2048,4096]{1,0:T(8,128)} %bitcast.55, f32[256,4096]{1,0:T(8,128)} %get-tuple-element.31, f32[256,4096]{1,0:T(8,128)} %get-tuple-element.32, f32[2048,512]{1,0:T(8,128)} %fusion.7, f32[2048]{0:T(1024)S(1)} %bitcast.65), kind=kOutput, calls=%fused_computation.4 | convolution fusion | flops 51559530496 | bytes 113254400 | tf_op jit(solution)/shard_map/dot_general | solution.py:103
  759.5 2.8 fusion.17
  762.3 2.8 fusion.18
  765.0 4.4 dynamic-slice_select_fusion.6
  769.5 0.0 all-reduce.10.cloned.1.call-start
  769.6 7.9 dynamic-slice_select_fusion.1
  777.6 0.6 copy-done.5
  778.2 5.0 broadcast_in_dim.165
  783.3 36.2 %copy.20 = f32[256,8,16,256]{3,1,2,0:T(8,128)} copy(f32[256,8,16,256]{3,2,1,0:T(8,128)S(1)} %bitcast.60) | data formatting | bytes 67108864
  819.5 0.1 broadcast_bitcast_fusion
  819.6 58.5 %all-reduce.14.cloned.1.call-done = (f32[2048,256]{1,0:T(8,128)}, f32[2048,256]{1,0:T(8,128)}) async-done(((f32[2048,256]{1,0:T(8,128)}, f32[2048,256]{1,0:T(8,128)}), (f32[2048,256]{1,0:T(8,128)}, f32[2048,256]{1,0:T(8,128)})) %all-reduce.14.cloned.1.call-update) | async-done | bytes 4194320 | tf_op jit(solution)/shard_map/psum | solution.py:14
  878.0 9.8 fusion.11
  887.8 145.9 %all-reduce.10.cloned.1.call-done = (f32[256,4096]{1,0:T(8,128)}, f32[256,4096]{1,0:T(8,128)}) async-done(((f32[256,4096]{1,0:T(8,128)}, f32[256,4096]{1,0:T(8,128)}), (f32[256,4096]{1,0:T(8,128)}, f32[256,4096]{1,0:T(8,128)})) %all-reduce.10.cloned.1.call-update) | async-done | bytes 8388624 | tf_op jit(solution)/shard_map/psum | solution.py:14
  1033.7 66.5 %multiply_subtract_fusion = f32[2048,4096]{1,0:T(8,128)} fusion(f32[2048,4096]{1,0:T(8,128)} %fusion.18, f32[2048,4096]{1,0:T(8,128)} %bitcast.56, f32[256,4096]{1,0:T(8,128)} %get-tuple-element.29, f32[256,4096]{1,0:T(8,128)} %get-tuple-element.30, f32[2048,512]{1,0:T(8,128)} %fusion.11, f32[2048]{0:T(1024)S(1)} %bitcast.67), kind=kOutput, calls=%fused_computation.3 | convolution fusion | flops 51559530496 | bytes 113254400 | tf_op jit(solution)/shard_map/dot_general | solution.py:103
  1100.2 2.8 fusion.19
  1103.1 23.0 %copy.37 = f32[1,2048,4096]{2,1,0:T(8,128)} copy(f32[1,2048,4096]{2,1,0:T(8,128)} %bitcast.54) | data formatting | bytes 67108864
  1126.1 2.8 fusion.21
  (45 shorter events, 0.3 us)
Async XLA Ops:
  6.5 158.1 %copy-start.9 = (s32[1,8]{1,0:T(1,128)S(1)}, s32[1,8]{1,0:T(1,128)}, u32[]{:S(2)}) copy-start(s32[1,8]{1,0:T(1,128)} %param.10) | copy-start | bytes 100
  6.5 165.9 %copy-start.6 = (s32[1,32]{1,0:T(1,128)S(1)}, s32[1,32]{1,0:T(1,128)}, u32[]{:S(2)}) copy-start(s32[1,32]{1,0:T(1,128)} %param.12) | copy-start | bytes 388
  6.5 154.8 %all-gather.5.cloned.1.call-start = ((), (), s32[]{:S(2)}) async-start(), calls=%async_computation | async-start | bytes 10485760 | tf_op jit(solution)/shard_map/all_gather | solution.py:37
  7.3 245.5 %all-gather.7.cloned.1.call-start = ((), (), s32[]{:S(2)}) async-start(), calls=%async_computation.1 | async-start | bytes 18874368 | tf_op jit(solution)/shard_map/all_gather | solution.py:58
  164.5 372.5 %all-reduce.16.cloned.1.call-start = ((), (), s32[]{:S(2)}) async-start(), calls=%async_computation.5 | async-start | bytes 8388608 | tf_op jit(solution)/shard_map/psum | solution.py:14
  179.7 6.2 copy-start.7
  181.1 4.8 copy-start.3
  427.9 265.0 %all-reduce.12.cloned.1.call-start = ((), (), s32[]{:S(2)}) async-start(), calls=%async_computation.3 | async-start | bytes 16777216 | tf_op jit(solution)/shard_map/psum | solution.py:14
  436.0 0.6 copy-start.10
  436.0 5.8 copy-start.4
  436.1 442.0 %all-reduce.14.cloned.1.call-start = ((), (), s32[]{:S(2)}) async-start(), calls=%async_computation.4 | async-start | bytes 8388608 | tf_op jit(solution)/shard_map/psum | solution.py:14
  447.2 89.9 %copy-start.2 = (f32[1,2,512,512]{3,2,1,0:T(8,128)S(1)}, f32[1,2,512,512]{3,2,1,0:T(8,128)}, u32[]{:S(2)}) copy-start(f32[1,2,512,512]{3,2,1,0:T(8,128)} %param.13) | copy-start | bytes 6291460
  692.9 66.5 %copy-start.1 = (f32[2048,512]{1,0:T(8,128)S(1)}, f32[2048,512]{1,0:T(8,128)}, u32[]{:S(2)}) copy-start(f32[2048,512]{1,0:T(8,128)} %fusion.7) | copy-start | bytes 12582916
  769.5 264.2 %all-reduce.10.cloned.1.call-start = ((), (), s32[]{:S(2)}) async-start(), calls=%async_computation.2 | async-start | bytes 16777216 | tf_op jit(solution)/shard_map/psum | solution.py:14
  777.6 0.7 copy-start.5
  783.3 36.2 %copy-start.8 = (f32[8]{0:T(128)S(1)}, f32[8]{0:T(128)}, u32[]{:S(2)}) copy-start(f32[8]{0:T(128)} %copy-done.7) | copy-start | bytes 100
  1033.7 66.5 %copy-start = (f32[2048,512]{1,0:T(8,128)S(1)}, f32[2048,512]{1,0:T(8,128)}, u32[]{:S(2)}) copy-start(f32[2048,512]{1,0:T(8,128)} %fusion.11) | copy-start | bytes 12582916
Sparse Core Ops, SparseCore 0:
  8.9 152.3 all-gather.4
  164.7 88.0 all-gather.6
  428.1 108.9 all-reduce.15
  539.7 153.2 all-reduce.11
  769.6 108.3 all-reduce.13
  880.5 153.2 all-reduce.9
where the time goes:
time: 1150 us; the launch traced here: 1140 us
  waiting for transfers between devices  576 us (50%)
  local copies, waits for them, and re-layouts  265 us (23%)
  matrix products  153 us (13%)
  other arithmetic  99.5 us (9%)
  between operations  25.3 us (2%)
  blocking collectives  17.7 us (2%)
    psum x4, waiting for transfers between devices, from_root(): return lax.psum(jnp.where(mine, x, jnp.zeros_like(x)), axis)  404 us
    unnamed x38, local copies, waits for them, and re-layouts  173 us
    all_gather x1, waiting for transfers between devices, body(): lax.all_gather(children, 'front', axis=0, tiled=True)  141 us
    dot_general x2, matrix products, body(): jnp.dot(lower * row_live[:, None], row_panel, precision=HIGH, preferred_e...  133 us
    mul x1, other arithmetic, body(): matrix = spread(mask_local) * (matrix_in + extended)  43.8 us
    reshape x2, local copies, waits for them, and re-layouts, body(): gathered.reshape(row_count, col_count, kid_count, kid_rows, BS, kid_cols,...  34.5 us
    all_gather x1, waiting for transfers between devices, body(): lax.all_gather(own_pieces[None], ('row', 'col'), axis=0, tiled=True)  30.5 us
    select_n x4, other arithmetic, from_root(): return lax.psum(jnp.where(mine, x, jnp.zeros_like(x)), axis)  24.9 us
  transfers between devices with their start and end apart: 6, of which 6 were waited for; matrix products, arithmetic and copies ran while one was open for 15% of the time, Pallas kernels for 0%

commit v1 on v0

v1 whole, which is shorter than its diff:
```python
import functools

import jax
import jax.numpy as jnp
from jax import lax
from jax.experimental import pallas as pl
from jax.experimental.pallas import tpu as pltpu
from jax.sharding import PartitionSpec as P

BS = 256
PIV = 4
HIGH = lax.Precision.HIGHEST


def split(x):
    hi = x.astype(jnp.bfloat16)
    return hi, (x - hi.astype(jnp.float32)).astype(jnp.bfloat16)


def dot(a, b):
    return jnp.dot(a, b, preferred_element_type=jnp.float32)


def dot3(a, b):
    ah, al = split(a)
    bh, bl = split(b)
    return dot(ah, bh) + (dot(al, bh) + dot(ah, bl))


def lower_kernel(meta, *refs, others, cols):
    cands = refs[: 1 + others]
    kids = refs[1 + others : 1 + others + PIV]
    diag, u01, hi_ref, lo_ref = refs[1 + others + PIV :]
    i = pl.program_id(0)
    parts = []
    for k in range(PIV):
        span = slice(k * BS, (k + 1) * BS)
        value = cands[0][:, span]
        for n in range(others):
            value = jnp.where(meta[0, k] == n + 1, cands[n + 1][:, span], value)
        kid = jnp.where(meta[2, k] * meta[4, i] == 1, kids[k][0, 0], 0.0)
        parts.append(jnp.where(meta[8 + k, i] == 1, value + kid, 0.0))
    low0 = dot3(jnp.concatenate(parts[:2], axis=1), diag[0, 0])
    change = dot3(low0, u01[...])
    nexts = [
        parts[2 + h] - jnp.where(meta[10 + h, i] == 1, change[:, h * BS : (h + 1) * BS], 0.0)
        for h in range(2)
    ]
    low1 = dot3(jnp.concatenate(nexts, axis=1), diag[0, 1])
    hi, lo = split(jnp.concatenate([low0, low1], axis=1))
    hi_ref[...] = hi
    lo_ref[...] = lo


def upper_kernel(meta, own, other, k0, k1, k2, k3, l10, hi_ref, lo_ref):
    j = pl.program_id(0)
    kids = (k0, k1, k2, k3)
    parts = []
    for k in range(PIV):
        value = jnp.where(meta[0, j] == 1, own[k], other[k])
        kid = jnp.where(meta[4, k] * meta[2, j] == 1, kids[k][0, 0], 0.0)
        parts.append(jnp.where(meta[8 + k, j] == 1, value + kid, 0.0))
    up0 = jnp.concatenate(parts[:2], axis=0)
    change = dot3(l10[...], up0)
    nexts = [
        parts[2 + h] - jnp.where(meta[10 + h, j] == 1, change[h * BS : (h + 1) * BS], 0.0)
        for h in range(2)
    ]
    hi, lo = split(jnp.concatenate([up0] + nexts, axis=0))
    hi_ref[...] = hi
    lo_ref[...] = lo


def trail_kernel(rows, cols, kinds, m_ref, slab, lh, ll, rh, rl, out, *, tile, kc):
    i = pl.program_id(0)
    t = pl.program_id(1)
    half = 2 * BS

    @pl.loop(0, tile)
    def _(n):
        j = t * tile + n
        kind = kinds[i, j]
        here = pl.ds(pl.multiple_of(n * BS, BS), BS)
        there = pl.ds(pl.multiple_of(j * BS, BS), BS)

        @pl.when(kind == 0)
        def _():
            out[:, here] = jnp.zeros((BS, BS), jnp.float32)

        def product(depth):
            ah, al = lh[:, :depth], ll[:, :depth]
            bh, bl = rh[:depth, there], rl[:depth, there]
            return dot(ah, bh) + dot(al, bh) + dot(ah, bl)

        @pl.when(kind == 1)
        def _():
            out[:, here] = m_ref[:, here]

        @pl.when(kind == 2)
        def _():
            out[:, here] = m_ref[:, here] - product(half)

        @pl.when(kind == 3)
        def _():
            out[:, here] = m_ref[:, here] - product(2 * half)

        @pl.when((kind >= 1) & (kind < 4) & (rows[0, i] * cols[0, j] == 1))
        def _():
            b = cols[1, j]
            span = pl.ds(pl.multiple_of(b % kc * BS, BS), BS)
            out[:, here] += slab[0, b // kc, :, span]

        @pl.when(kind >= 4)
        def _():
            span = pl.ds(pl.multiple_of((kind - 4) * BS, BS), BS)
            out[:, here] = lh[:, span].astype(jnp.float32) + ll[:, span].astype(jnp.float32)


def body(front_orig, children, parent_of, child_map, block_mask, pivot, diag_inverse):
    f32, i32 = jnp.float32, jnp.int32
    nrow, ncol = lax.axis_size("row"), lax.axis_size("col")
    r, c = lax.axis_index("row"), lax.axis_index("col")
    matrix = front_orig[0]
    loc_rows, loc_cols = matrix.shape
    rb, cb = loc_rows // BS, loc_cols // BS
    kr, kc = children.shape[1] // BS, children.shape[2] // BS
    nb = block_mask.shape[1]
    order = pivot[0]
    mask = block_mask[0]

    col_slot = [order[k] % cb for k in range(PIV)]
    row_slot = [order[k] % rb for k in range(PIV)]
    mine_c = jnp.concatenate(
        [lax.dynamic_slice(matrix, (0, col_slot[k] * BS), (loc_rows, BS)) for k in range(PIV)], axis=1
    )
    cands = [mine_c] + [
        lax.ppermute(mine_c, "col", [(s, (s + n) % ncol) for s in range(ncol)]) for n in range(1, ncol)
    ]

    core = r % 2
    wide = loc_cols // 2
    near = [(s, s ^ 1) for s in range(nrow)]
    halves, others = [], []
    for k in range(PIV):
        owner = order[k] // rb
        start = row_slot[k] * BS
        give = lax.dynamic_slice(matrix, (start, (1 - core) * wide), (BS, wide))
        keep = lax.dynamic_slice(matrix, (start, core * wide), (BS, wide))
        got = lax.ppermute(give, "row", near)
        part = jnp.where(owner % 2 == core, keep, got)
        hop = 2
        while hop < nrow:
            got = lax.ppermute(part, "row", [(s, s ^ hop) for s in range(nrow)])
            part = jnp.where((owner // hop) % 2 == (r // hop) % 2, part, got)
            hop *= 2
        halves.append(part)
        others.append(lax.ppermute(part, "row", near))
    half_own, half_other = jnp.stack(halves), jnp.stack(others)

    parents = lax.all_gather(parent_of, "front", axis=0, tiled=True)
    maps = lax.all_gather(child_map, "front", axis=0, tiled=True)
    pieces = lax.all_gather(children, "front", axis=0, tiled=True)
    owned = jnp.argmax((parents == lax.axis_index("front")).astype(i32)).astype(i32)
    own_map = lax.dynamic_index_in_dim(maps, owned, 0, keepdims=False)
    piece = lax.dynamic_index_in_dim(pieces, owned, 0, keepdims=True)
    kid = lax.all_gather(piece, ("row", "col"), axis=0, tiled=True)
    kid = kid.reshape(nrow, ncol, kr * BS, kc * BS)

    ids = jnp.arange(nb, dtype=i32)
    has = jnp.any(own_map[:, None] == ids[None, :], axis=0).astype(i32)
    src = jnp.maximum(jnp.sum((own_map[:, None] <= ids[None, :]).astype(i32), axis=0) - 1, 0)
    position = jnp.sum(jnp.where(order[:, None] == ids[None, :], ids[:, None], 0), axis=0).astype(i32)

    def rows_of(x):
        return lax.dynamic_slice_in_dim(x, r * rb, rb)

    def cols_of(x):
        return lax.dynamic_slice_in_dim(x, c * cb, cb)

    def picked(x):
        hit = (order[:PIV, None] == ids[None, :]).astype(i32)
        return jnp.sum(hit * x[None, :], axis=1)

    hit = (order[:PIV, None] == ids[None, :]).astype(i32)
    mask_cols = jnp.sum(hit[:, :, None] * mask.T[None], axis=1)
    mask_rows = jnp.sum(hit[:, :, None] * mask[None], axis=1)
    pos_r, pos_c = rows_of(position)[:, None], cols_of(position)[None, :]
    local_mask = lax.dynamic_slice(mask, (r * rb, c * cb), (rb, cb))
    kinds = jnp.where((pos_r >= 2) & (pos_c >= 2), 2, 1)
    kinds = jnp.where((pos_r >= 4) & (pos_c >= 4), 3, kinds)
    kinds = jnp.where(local_mask > 0, kinds, 0)
    kinds = jnp.where((pos_c < PIV) & (pos_r >= pos_c // 2 * 2 + 2), 4 + pos_c, kinds).astype(i32)

    def corner(x, y):
        orr, occ = order[x], order[y]
        block = lax.dynamic_slice(matrix, (row_slot[x] * BS, col_slot[y] * BS), (BS, BS))
        return jnp.where((orr // rb == r) & (occ // cb == c), block, 0.0)

    def square(make, xs, ys):
        return jnp.concatenate([jnp.concatenate([make(x, y) for y in ys], axis=1) for x in xs], axis=0)

    corners = lax.psum(
        jnp.stack([square(corner, (0, 1), (2, 3)), square(corner, (2, 3), (0, 1))]), ("row", "col")
    )
    psrc, phas = picked(src), picked(has)

    def kid_corner(x, y):
        a, b = psrc[x], psrc[y]
        block = lax.dynamic_slice(kid, (a // kr, b // kc, a % kr * BS, b % kc * BS), (1, 1, BS, BS))
        return jnp.where(phas[x] * phas[y] == 1, block[0, 0], 0.0)

    def mask_corner(x, y):
        return jnp.broadcast_to(picked(mask_rows[x])[y], (BS, BS)).astype(f32)

    u01 = (corners[0] + square(kid_corner, (0, 1), (2, 3))) * square(mask_corner, (0, 1), (2, 3))
    a10 = (corners[1] + square(kid_corner, (2, 3), (0, 1))) * square(mask_corner, (2, 3), (0, 1))
    l10 = jnp.dot(a10, diag_inverse[0, 0], precision=HIGH, preferred_element_type=f32)

    def pad(rows, n):
        return jnp.pad(rows.astype(i32), (0, n - rows.shape[0]))

    n = max(rb, PIV)
    zero = jnp.zeros((n,), i32)
    shift = jnp.stack([(c - order[k] // cb) % ncol for k in range(PIV)])
    meta = jnp.stack(
        [pad(shift, n), pad(psrc, n), pad(phas, n), pad(rows_of(src), n), pad(rows_of(has), n)]
        + [zero] * 3
        + [pad(rows_of(mask_cols[k]), n) for k in range(PIV)]
    )
    params = pltpu.CompilerParams(vmem_limit_bytes=52 * 2**20)

    def kid_spec(k):
        def where(i, m):
            a, b = m[3, i], m[1, k]
            return a // kr, b // kc, a % kr, b % kc

        return pl.BlockSpec((1, 1, BS, BS), where)

    low_h, low_l = pl.pallas_call(
        functools.partial(lower_kernel, others=ncol - 1, cols=cb),
        grid_spec=pltpu.PrefetchScalarGridSpec(
            num_scalar_prefetch=1,
            grid=(rb,),
            in_specs=[pl.BlockSpec((BS, PIV * BS), lambda i, m: (i, 0))] * ncol
            + [kid_spec(k) for k in range(PIV)]
            + [
                pl.BlockSpec((1, 2, 2 * BS, 2 * BS), lambda i, m: (0, 0, 0, 0)),
                pl.BlockSpec((2 * BS, 2 * BS), lambda i, m: (0, 0)),
            ],
            out_specs=[pl.BlockSpec((BS, PIV * BS), lambda i, m: (i, 0))] * 2,
        ),
        out_shape=[jax.ShapeDtypeStruct((loc_rows, PIV * BS), jnp.bfloat16)] * 2,
        compiler_params=params,
        name="lower",
    )(meta, *cands, *[kid] * PIV, diag_inverse, u01)

    n = max(cb, PIV)
    zero = jnp.zeros((n,), i32)
    held = (jnp.arange(cb, dtype=i32) // (cb // 2) == core).astype(i32)
    meta = jnp.stack(
        [pad(held, n), pad(cols_of(src), n), pad(cols_of(has), n), pad(psrc, n), pad(phas, n)]
        + [zero] * 3
        + [pad(cols_of(mask_rows[k]), n) for k in range(PIV)]
    )

    def kid_spec_up(k):
        def where(j, m):
            a, b = m[3, k], m[1, j]
            return a // kr, b // kc, a % kr, b % kc

        return pl.BlockSpec((1, 1, BS, BS), where)

    up_h, up_l = pl.pallas_call(
        upper_kernel,
        grid_spec=pltpu.PrefetchScalarGridSpec(
            num_scalar_prefetch=1,
            grid=(cb,),
            in_specs=[pl.BlockSpec((PIV, BS, BS), lambda j, m: (0, 0, j % (cb // 2)))] * 2
            + [kid_spec_up(k) for k in range(PIV)]
            + [pl.BlockSpec((2 * BS, 2 * BS), lambda j, m: (0, 0))],
            out_specs=[pl.BlockSpec((PIV * BS, BS), lambda j, m: (0, j))] * 2,
        ),
        out_shape=[jax.ShapeDtypeStruct((PIV * BS, loc_cols), jnp.bfloat16)] * 2,
        compiler_params=params,
        name="upper",
    )(meta, half_own, half_other, *[kid] * PIV, l10)

    tile = min(4, cb)
    rows = jnp.stack([rows_of(has), rows_of(src)])
    cols = jnp.stack([cols_of(has), cols_of(src)])
    out = pl.pallas_call(
        functools.partial(trail_kernel, tile=tile, kc=kc),
        grid_spec=pltpu.PrefetchScalarGridSpec(
            num_scalar_prefetch=3,
            grid=(rb, cb // tile),
            in_specs=[
                pl.BlockSpec((BS, tile * BS), lambda i, t, rows, *_: (i, t)),
                pl.BlockSpec(
                    (1, ncol, BS, kc * BS), lambda i, t, rows, *_: (rows[1, i] // kr, 0, rows[1, i] % kr, 0)
                ),
                pl.BlockSpec((BS, PIV * BS), lambda i, t, *_: (i, 0)),
                pl.BlockSpec((BS, PIV * BS), lambda i, t, *_: (i, 0)),
                pl.BlockSpec(memory_space=pltpu.VMEM),
                pl.BlockSpec(memory_space=pltpu.VMEM),
            ],
            out_specs=pl.BlockSpec((BS, tile * BS), lambda i, t, *_: (i, t)),
        ),
        out_shape=jax.ShapeDtypeStruct((loc_rows, loc_cols), f32),
        compiler_params=params,
        name="trail",
    )(rows, cols, kinds, matrix, kid, low_h, low_l, up_h, up_l)
    return out[None]


def solution(mesh):
    placed = (
        P("front", "row", "col"),
        P("front", "row", "col"),
        P("front"),
        P("front", None),
        P("front", None, None),
        P("front", None),
        P("front", None, None, None),
    )
    return jax.shard_map(
        body, mesh=mesh, in_specs=placed, out_specs=P("front", "row", "col"), check_vma=False
    )
```

time: 1150 us -> 613 us (0.53)
  local copies, waits for them, and re-layouts: 265 us -> 21.4 us
  waiting for transfers between devices: 576 us -> 346 us
  matrix products: 153 us -> 3.5 us
  Pallas kernels: 0 us -> 118 us
  other arithmetic: 99.5 us -> 47.1 us
  between operations: 25.3 us -> 46.1 us
    psum x4 -> x1, waiting for transfers between devices: 404 us -> 0.02 us  [body(): lax.psum(jnp.stack([square(corner, (0, 1), (2, 3)), square(corner, (2, 3)...]
    ppermute x0 -> x13, waiting for transfers between devices: none -> 205 us  [the longest x4 205 us: body(): got = lax.ppermute(part, 'row', [(s, s ^ hop) for s in range(nrow)])]
    unnamed x38 -> x17, local copies, waits for them, and re-layouts: 173 us -> 2.96 us
    dot_general x4 -> x1, matrix products: 153 us -> 3.5 us  [body(): jnp.dot(a10, diag_inverse[0, 0], precision=HIGH, preferred_element_type=f32)]
    pallas_call x0 -> x3, Pallas kernels: none -> 118 us  [the longest x1 72.6 us: body(): pl.pallas_call(functools.partial(trail_kernel, tile=tile, kc=kc), grid_sp...]
    mul x4 -> x1, other arithmetic: 45.3 us -> 0.3 us  [body(): (corners[0] + square(kid_corner, (0, 1), (2, 3))) * square(mask_corner, (...]
    reshape x2 -> x0, local copies, waits for them, and re-layouts: 34.5 us -> none  [body(): gathered.reshape(row_count, col_count, kid_count, kid_rows, BS, kid_cols,...]
    all_gather x2, waiting for transfers between devices: 171 us -> 140 us  [the longest x1 140 us: body(): pieces = lax.all_gather(children, 'front', axis=0, tiled=True)]
  transfers between devices with their start and end apart: 6 -> 16, of which waited for: 6 -> 5; matrix products, arithmetic and copies ran while one was open for 15% -> 11% of each run, Pallas kernels for 0% -> 4%
where the time goes in v1:
time: 613 us; the launch traced here: 607 us
  waiting for transfers between devices  346 us (56%)
  Pallas kernels  118 us (19%)
  other arithmetic  47.1 us (8%)
  between operations  46.1 us (8%)
  local copies, waits for them, and re-layouts  21.4 us (3%)
  blocking collectives  18.7 us (3%)
  starting transfers between devices  6.83 us (1%)
    ppermute x4, waiting for transfers between devices, body(): got = lax.ppermute(part, 'row', [(s, s ^ hop) for s in range(nrow)])  205 us
    all_gather x1, waiting for transfers between devices, body(): pieces = lax.all_gather(children, 'front', axis=0, tiled=True)  140 us
    pallas_call x1, Pallas kernels, body(): pl.pallas_call(functools.partial(trail_kernel, tile=tile, kc=kc), grid_sp...  72.6 us
    pallas_call x1, Pallas kernels, body(): pl.pallas_call(upper_kernel, grid_spec=pltpu.PrefetchScalarGridSpec(num_s...  26.1 us
    pallas_call x1, Pallas kernels, body(): pl.pallas_call(functools.partial(lower_kernel, others=ncol - 1, cols=cb),...  18.9 us
    select_n x4, other arithmetic, body(): part = jnp.where(owner // hop % 2 == r // hop % 2, part, got)  13 us
  transfers between devices with their start and end apart: 16, of which 5 were waited for; matrix products, arithmetic and copies ran while one was open for 11% of the time, Pallas kernels for 4%

profile of v1, /device:TPU:0, one launch (start us, length us, event | category | flops | bytes accessed | tf_op | source)
XLA Modules:
  0.0 606.7 jit_solution(369589038484516067)
XLA Ops:
  6.5 0.7 all-gather.4.cloned.1.call-update
  8.0 0.6 dynamic-slice.29
  8.6 0.8 dynamic-update-slice
  9.3 9.9 %all-reduce.9 = s32[4]{0:T(128)S(1)} all-reduce(s32[4]{0:T(128)S(1)} %dynamic-update-slice), channel_id=1, replica_groups=mesh['front'=4,'row'=4,'col'=2] {'front'}, use_global_device_ids=true, to_apply=%add.9 | all-reduce | flops 4 | bytes 32
  19.2 0.7 fusion.18
  21.8 139.5 %all-gather.4.cloned.1.call-done = f32[4,512,1024]{2,1,0:T(8,128)} async-done(((f32[1,512,1024]{2,1,0:T(8,128)}), f32[4,512,1024]{2,1,0:T(8,128)}) %all-gather.4.cloned.1.call-update) | async-done | bytes 8388624 | tf_op jit(solution)/shard_map/all_gather | solution.py:162
  161.3 3.2 constant_dynamic-slice_fusion.8
  164.6 0.6 copy-done.4
  165.2 0.6 fusion.29
  173.0 7.7 %dynamic-slice_bitcast_fusion.3 = (f32[256,2048]{1,0:T(8,128)}, f32[256,2048]{1,0:T(8,128)}, f32[256,2048]{1,0:T(8,128)}, f32[256,2048]{1,0:T(8,128)}) fusion(f32[1,2048,4096]{2,1,0:T(8,128)} %param.7, s32[]{:T(128)S(6)} %select_n.644, s32[]{:T(128)S(6)} %select_n.715, s32[]{:T(128)S(6)} %select_n.662, s32[]{:T(128)S(6)} %select_n.653, s32[]{:T(128)S(6)} %select_n.671), kind=kLoop, calls=%fused_computation.11 | loop fusion | bytes 16777236 | tf_op jit(solution)/shard_map/dynamic_slice | solution.py:147
  180.7 0.1 collective-permute-start.1
  180.8 0.4 collective-permute-start.5
  181.2 0.1 collective-permute-start.3
  181.3 0.4 collective-permute-start.7
  181.7 4.1 dynamic-slice_bitcast_fusion.7
  185.8 4.0 pad_maximum_fusion.refs_0_
  189.7 1.5 collective-permute-start
  193.8 1.7 select_bitcast_fusion.15
  195.5 0.3 maximum_bitcast_fusion
  195.8 1.5 pad_maximum_fusion.3
  197.3 0.6 copy-done.5
  197.9 8.8 %all-gather = s32[4,1,8]{2,1,0:T(1,128)S(1)} all-gather(s32[1,1,8]{2,1,0:T(1,128)S(1)} %bitcast.166), channel_id=1, replica_groups=mesh['front'=4,'row'=4,'col'=2] {'front'}, dimensions={0}, use_global_device_ids=true | all-gather | bytes 160 | tf_op jit(solution)/shard_map/all_gather | solution.py:161
  206.7 0.1 convert_reduce_fusion
  206.8 0.1 fusion.17
  206.9 10.0 %bitcast_select_fusion.3 = (f32[256,2048]{1,0:T(8,128)}, f32[256,2048]{1,0:T(8,128)}, f32[256,2048]{1,0:T(8,128)}, f32[256,2048]{1,0:T(8,128)S(1)}) fusion(f32[256,2048]{1,0:T(8,128)} %collective-permute-done.1, f32[1,2048,4096]{2,1,0:T(8,128)} %param.7, s32[]{:T(128)S(6)} %select_n.644, s32[]{:T(128)S(6)} %select_n.714, pred[]{:T(512)S(6)} %eq.302, ...), kind=kLoop, calls=%fused_computation.7 | loop fusion | flops 2097152 | bytes 25165848 | tf_op jit(solution)/shard_map/jit(_where)/select_n | solution.py:150
  216.9 1.1 collective-permute-start.2
  218.0 0.1 fusion.15
  218.2 0.1 multiply_reduce_fusion
  218.3 0.2 select_reduce_fusion.2
  218.6 1.0 collective-permute-start.6
  219.6 0.1 dynamic-slice_bitcast_fusion.8
  219.7 0.1 constant_dynamic-slice_fusion
  219.7 0.1 constant_dynamic-slice_fusion.2
  219.8 0.7 fusion.23
  220.5 1.1 collective-permute-start.4
  221.6 0.7 fusion.25
  222.2 0.7 fusion.27
  222.9 1.0 collective-permute-start.8
  223.9 0.1 pad_add_fusion.2
  244.5 0.1 dynamic-slice_bitcast_fusion.10
  244.6 0.1 constant_dynamic-slice_fusion.4
  244.6 58.9 %collective-permute-done.2 = f32[256,2048]{1,0:T(8,128)} collective-permute-done((f32[256,2048]{1,0:T(8,128)}, f32[256,2048]{1,0:T(8,128)}, u32[]{:S(2)}, u32[]{:S(2)}) %collective-permute-start.2) | collective-permute-done | bytes 2097184 | tf_op jit(solution)/shard_map/ppermute | solution.py:153
  303.5 3.3 broadcast_select_fusion.3
  306.8 55.7 %collective-permute-done.6 = f32[256,2048]{1,0:T(8,128)} collective-permute-done((f32[256,2048]{1,0:T(8,128)}, f32[256,2048]{1,0:T(8,128)}, u32[]{:S(2)}, u32[]{:S(2)}) %collective-permute-start.6) | collective-permute-done | bytes 2097184 | tf_op jit(solution)/shard_map/ppermute | solution.py:153
  362.5 3.2 broadcast_select_fusion.1
  365.7 50.2 %collective-permute-done.4 = f32[256,2048]{1,0:T(8,128)} collective-permute-done((f32[256,2048]{1,0:T(8,128)}, f32[256,2048]{1,0:T(8,128)}, u32[]{:S(2)}, u32[]{:S(2)}) %collective-permute-start.4) | collective-permute-done | bytes 2097184 | tf_op jit(solution)/shard_map/ppermute | solution.py:153
  415.9 3.3 broadcast_select_fusion.2
  419.2 40.5 %collective-permute-done.8 = f32[256,2048]{1,0:T(8,128)} collective-permute-done((f32[256,2048]{1,0:T(8,128)S(1)}, f32[256,2048]{1,0:T(8,128)}, u32[]{:S(2)}, u32[]{:S(2)}) %collective-permute-start.8) | collective-permute-done | bytes 2097184 | tf_op jit(solution)/shard_map/ppermute | solution.py:153
  459.7 3.3 broadcast_select_fusion
  462.9 0.1 constant_dynamic-slice_fusion.6
  463.0 0.1 select_reduce_fusion
  463.1 0.1 broadcast_compare_fusion.1
  463.2 0.1 broadcast_compare_fusion.4
  463.4 0.1 select_select_fusion.kinds
  463.4 5.9 pad_maximum_fusion.1.own
  469.4 5.9 pad_maximum_fusion.2.other
  475.2 1.5 select_bitcast_fusion.3
  477.0 3.5 fusion.2.l10
  480.5 26.1 %upper.1 = (bf16[1024,4096]{1,0:T(8,128)(2,1)}, bf16[1024,4096]{1,0:T(8,128)(2,1)}) custom-call(s32[12,16]{1,0:T(8,128)S(1)} %stack.130.meta, f32[4,256,2048]{2,1,0:T(8,128)} %pad_maximum_fusion.1.own, f32[4,256,2048]{2,1,0:T(8,128)} %pad_maximum_fusion.2.other, f32[4,2,512,1024]{3,2,1,0:T(8,128)} %bitcast.152, f32[4,2,512,1024]{3,2,1,0:T(8,128)} %bitcast.153, ...), custom_call_target="tpu_custom_call" | custom-call | tf_op jit(solution)/shard_map/upper/pallas_call | solution.py:273
  506.6 1.2 select_bitcast_fusion.7
  507.9 0.4 copy-done.2
  508.3 0.3 fusion.5.refs_7_
  508.7 18.9 %lower.1 = (bf16[2048,1024]{1,0:T(8,128)(2,1)}, bf16[2048,1024]{1,0:T(8,128)(2,1)}) custom-call(s32[12,8]{1,0:T(8,128)S(1)} %stack.123.meta, f32[2048,1024]{1,0:T(8,128)} %pad_maximum_fusion.refs_0_, f32[2048,1024]{1,0:T(8,128)} %collective-permute-done.refs_1_, f32[4,2,512,1024]{3,2,1,0:T(8,128)} %bitcast.157, f32[4,2,512,1024]{3,2,1,0:T(8,128)} %bitcast.158, ...), custom_call_target="tpu_custom_call" | custom-call | tf_op jit(solution)/shard_map/lower/pallas_call | solution.py:239
  527.6 72.6 %trail.1 = f32[2048,4096]{1,0:T(8,128)} custom-call(s32[2,8]{1,0:T(2,128)S(1)} %pad_add_fusion.rows, s32[2,16]{1,0:T(2,128)S(1)} %pad_add_fusion.1.cols, s32[8,16]{1,0:T(8,128)S(1)} %select_select_fusion.kinds, f32[2048,4096]{1,0:T(8,128)} %bitcast.162, f32[4,2,512,1024]{3,2,1,0:T(8,128)} %bitcast.161, bf16[2048,1024]{1,0:T(8,128)(2,1)} %get-tuple-element.11.lh, ...), custom_call_target="tpu_custom_call" | custom-call | tf_op jit(solution)/shard_map/trail/pallas_call | solution.py:291
  (68 shorter events, 0.8 us)
Async XLA Ops:
  6.5 1.4 copy-start.6
  6.5 154.8 %all-gather.4.cloned.1.call-start = ((), (), s32[]{:S(2)}) async-start(), calls=%async_computation | async-start | bytes 10485760 | tf_op jit(solution)/shard_map/all_gather | solution.py:162
  7.3 468.0 %all-gather.6.cloned.1.call-start = ((), (), s32[]{:S(2)}) async-start(), calls=%async_computation.1 | async-start | bytes 18874368 | tf_op jit(solution)/shard_map/all_gather | solution.py:166
  164.5 0.7 copy-start.4
  164.5 312.3 %all-reduce.12.cloned.1.call-start = ((), (), s32[]{:S(2)}) async-start(), calls=%async_computation.2 | async-start | bytes 4194304 | tf_op jit(solution)/shard_map/psum | solution.py:202
  180.7 26.2 %collective-permute-start.1 = (f32[256,2048]{1,0:T(8,128)}, f32[256,2048]{1,0:T(8,128)}, u32[]{:S(2)}, u32[]{:S(2)}) collective-permute-start(f32[256,2048]{1,0:T(8,128)} %get-tuple-element.31), channel_id=1, source_target_pairs={{0,2},{2,0},{4,6},{6,4},{1,3},{3,1},{5,7},{7,5},{8,10},{10,8},{12,... | collective-permute-start | bytes 6291464 | tf_op jit(solution)/shard_map/ppermute | solution.py:149
  180.8 26.1 %collective-permute-start.5 = (f32[256,2048]{1,0:T(8,128)}, f32[256,2048]{1,0:T(8,128)}, u32[]{:S(2)}, u32[]{:S(2)}) collective-permute-start(f32[256,2048]{1,0:T(8,128)} %get-tuple-element.32), channel_id=1, source_target_pairs={{0,2},{2,0},{4,6},{6,4},{1,3},{3,1},{5,7},{7,5},{8,10},{10,8},{12,... | collective-permute-start | bytes 6291464 | tf_op jit(solution)/shard_map/ppermute | solution.py:149
  181.2 25.7 %collective-permute-start.3 = (f32[256,2048]{1,0:T(8,128)}, f32[256,2048]{1,0:T(8,128)}, u32[]{:S(2)}, u32[]{:S(2)}) collective-permute-start(f32[256,2048]{1,0:T(8,128)} %get-tuple-element.33), channel_id=1, source_target_pairs={{0,2},{2,0},{4,6},{6,4},{1,3},{3,1},{5,7},{7,5},{8,10},{10,8},{12,... | collective-permute-start | bytes 6291464 | tf_op jit(solution)/shard_map/ppermute | solution.py:149
  181.3 25.6 %collective-permute-start.7 = (f32[256,2048]{1,0:T(8,128)}, f32[256,2048]{1,0:T(8,128)}, u32[]{:S(2)}, u32[]{:S(2)}) collective-permute-start(f32[256,2048]{1,0:T(8,128)} %get-tuple-element.34), channel_id=1, source_target_pairs={{0,2},{2,0},{4,6},{6,4},{1,3},{3,1},{5,7},{7,5},{8,10},{10,8},{12,... | collective-permute-start | bytes 6291464 | tf_op jit(solution)/shard_map/ppermute | solution.py:149
  189.7 318.9 %collective-permute-start = (f32[2048,1024]{1,0:T(8,128)}, f32[2048,1024]{1,0:T(8,128)}, u32[]{:S(2)}, u32[]{:S(2)}) collective-permute-start(f32[2048,1024]{1,0:T(8,128)} %pad_maximum_fusion.refs_0_), channel_id=1, source_target_pairs={{0,1},{1,0},{2,3},{3,2},{4,5},{5,4},{6,7},{7,6},{8,9},{9,8},{10,11... | collective-permute-start | bytes 25165832 | tf_op jit(solution)/shard_map/ppermute | solution.py:137
  197.3 0.7 copy-start.5
  206.9 11.3 %copy-start.3 = (s32[1,32,32]{2,1,0:T(8,128)S(1)}, s32[1,32,32]{2,1,0:T(8,128)}, u32[]{:S(2)}) copy-start(s32[1,32,32]{2,1,0:T(8,128)} %param.11) | copy-start | bytes 12292
  216.9 86.6 %collective-permute-start.2 = (f32[256,2048]{1,0:T(8,128)}, f32[256,2048]{1,0:T(8,128)}, u32[]{:S(2)}, u32[]{:S(2)}) collective-permute-start(f32[256,2048]{1,0:T(8,128)} %get-tuple-element.27), channel_id=1, source_target_pairs={{0,4},{2,6},{4,0},{6,2},{1,5},{3,7},{5,1},{7,3},{8,12},{10,14},{12... | collective-permute-start | bytes 6291464 | tf_op jit(solution)/shard_map/ppermute | solution.py:153
  218.6 144.0 %collective-permute-start.6 = (f32[256,2048]{1,0:T(8,128)}, f32[256,2048]{1,0:T(8,128)}, u32[]{:S(2)}, u32[]{:S(2)}) collective-permute-start(f32[256,2048]{1,0:T(8,128)} %get-tuple-element.28), channel_id=1, source_target_pairs={{0,4},{2,6},{4,0},{6,2},{1,5},{3,7},{5,1},{7,3},{8,12},{10,14},{12... | collective-permute-start | bytes 6291464 | tf_op jit(solution)/shard_map/ppermute | solution.py:153
  220.5 195.4 %collective-permute-start.4 = (f32[256,2048]{1,0:T(8,128)}, f32[256,2048]{1,0:T(8,128)}, u32[]{:S(2)}, u32[]{:S(2)}) collective-permute-start(f32[256,2048]{1,0:T(8,128)} %get-tuple-element.29), channel_id=1, source_target_pairs={{0,4},{2,6},{4,0},{6,2},{1,5},{3,7},{5,1},{7,3},{8,12},{10,14},{12... | collective-permute-start | bytes 6291464 | tf_op jit(solution)/shard_map/ppermute | solution.py:153
  222.9 236.7 %collective-permute-start.8 = (f32[256,2048]{1,0:T(8,128)S(1)}, f32[256,2048]{1,0:T(8,128)}, u32[]{:S(2)}, u32[]{:S(2)}) collective-permute-start(f32[256,2048]{1,0:T(8,128)S(1)} %get-tuple-element.30), channel_id=1, source_target_pairs={{0,4},{2,6},{4,0},{6,2},{1,5},{3,7},{5,1},{7,3},{8,12},{10,14},{12... | collective-permute-start | bytes 6291464 | tf_op jit(solution)/shard_map/ppermute | solution.py:153
  244.6 117.9 %copy-start.1 = (f32[256,2048]{1,0:T(8,128)S(1)}, f32[256,2048]{1,0:T(8,128)}, u32[]{:S(2)}) copy-start(f32[256,2048]{1,0:T(8,128)} %get-tuple-element.28) | copy-start | bytes 6291460
  306.8 109.1 %copy-start = (f32[256,2048]{1,0:T(8,128)S(1)}, f32[256,2048]{1,0:T(8,128)}, u32[]{:S(2)}) copy-start(f32[256,2048]{1,0:T(8,128)} %get-tuple-element.29) | copy-start | bytes 6291460
  306.8 162.5 %collective-permute-start.9 = (f32[256,2048]{1,0:T(8,128)}, f32[256,2048]{1,0:T(8,128)}, u32[]{:S(2)}, u32[]{:S(2)}) collective-permute-start(f32[256,2048]{1,0:T(8,128)} %broadcast_select_fusion.3), channel_id=1, source_target_pairs={{0,2},{2,0},{4,6},{6,4},{1,3},{3,1},{5,7},{7,5},{8,10},{10,8},{12,... | collective-permute-start | bytes 6291464 | tf_op jit(solution)/shard_map/ppermute | solution.py:157
  365.7 103.6 %collective-permute-start.11 = (f32[256,2048]{1,0:T(8,128)}, f32[256,2048]{1,0:T(8,128)}, u32[]{:S(2)}, u32[]{:S(2)}) collective-permute-start(f32[256,2048]{1,0:T(8,128)} %broadcast_select_fusion.1), channel_id=1, source_target_pairs={{0,2},{2,0},{4,6},{6,4},{1,3},{3,1},{5,7},{7,5},{8,10},{10,8},{12,... | collective-permute-start | bytes 6291464 | tf_op jit(solution)/shard_map/ppermute | solution.py:157
  419.2 50.2 %collective-permute-start.10 = (f32[256,2048]{1,0:T(8,128)}, f32[256,2048]{1,0:T(8,128)}, u32[]{:S(2)}, u32[]{:S(2)}) collective-permute-start(f32[256,2048]{1,0:T(8,128)} %broadcast_select_fusion.2), channel_id=1, source_target_pairs={{0,2},{2,0},{4,6},{6,4},{1,3},{3,1},{5,7},{7,5},{8,10},{10,8},{12,... | collective-permute-start | bytes 6291464 | tf_op jit(solution)/shard_map/ppermute | solution.py:157
  462.9 6.4 %collective-permute-start.12 = (f32[256,2048]{1,0:T(8,128)}, f32[256,2048]{1,0:T(8,128)}, u32[]{:S(2)}, u32[]{:S(2)}) collective-permute-start(f32[256,2048]{1,0:T(8,128)} %broadcast_select_fusion), channel_id=1, source_target_pairs={{0,2},{2,0},{4,6},{6,4},{1,3},{3,1},{5,7},{7,5},{8,10},{10,8},{12,... | collective-permute-start | bytes 6291464 | tf_op jit(solution)/shard_map/ppermute | solution.py:157
  506.6 1.8 copy-start.2
Sparse Core Ops, SparseCore 0:
  8.9 152.3 all-gather.3
  164.6 140.2 all-gather.5
  308.2 80.7 all-reduce.11

commit v2 on v1

--- a/solution.py
+++ b/solution.py
@@ -28,16 +28,15 @@
 
 
 def lower_kernel(meta, *refs, others, cols):
-    cands = refs[: 1 + others]
-    kids = refs[1 + others : 1 + others + PIV]
-    diag, u01, hi_ref, lo_ref = refs[1 + others + PIV :]
+    cands = refs[: (1 + others) * PIV]
+    kids = refs[(1 + others) * PIV : (2 + others) * PIV]
+    diag, u01, hi_ref, lo_ref = refs[(2 + others) * PIV :]
     i = pl.program_id(0)
     parts = []
     for k in range(PIV):
-        span = slice(k * BS, (k + 1) * BS)
-        value = cands[0][:, span]
-        for n in range(others):
-            value = jnp.where(meta[0, k] == n + 1, cands[n + 1][:, span], value)
+        value = cands[k][...]
+        for n in range(1, others + 1):
+            value = jnp.where(meta[0, k] == n, cands[n * PIV + k][...], value)
         kid = jnp.where(meta[2, k] * meta[4, i] == 1, kids[k][0, 0], 0.0)
         parts.append(jnp.where(meta[8 + k, i] == 1, value + kid, 0.0))
     low0 = dot3(jnp.concatenate(parts[:2], axis=1), diag[0, 0])
@@ -52,12 +51,13 @@
     lo_ref[...] = lo
 
 
-def upper_kernel(meta, own, other, k0, k1, k2, k3, l10, hi_ref, lo_ref):
+def upper_kernel(meta, *refs):
+    own, other, kids = refs[:PIV], refs[PIV : 2 * PIV], refs[2 * PIV : 3 * PIV]
+    l10, hi_ref, lo_ref = refs[3 * PIV :]
     j = pl.program_id(0)
-    kids = (k0, k1, k2, k3)
     parts = []
     for k in range(PIV):
-        value = jnp.where(meta[0, j] == 1, own[k], other[k])
+        value = jnp.where(meta[0, j] == 1, own[k][...], other[k][...])
         kid = jnp.where(meta[4, k] * meta[2, j] == 1, kids[k][0, 0], 0.0)
         parts.append(jnp.where(meta[8 + k, j] == 1, value + kid, 0.0))
     up0 = jnp.concatenate(parts[:2], axis=0)
@@ -130,11 +130,10 @@
 
     col_slot = [order[k] % cb for k in range(PIV)]
     row_slot = [order[k] % rb for k in range(PIV)]
-    mine_c = jnp.concatenate(
-        [lax.dynamic_slice(matrix, (0, col_slot[k] * BS), (loc_rows, BS)) for k in range(PIV)], axis=1
-    )
+    mine_c = [lax.dynamic_slice(matrix, (0, col_slot[k] * BS), (loc_rows, BS)) for k in range(PIV)]
     cands = [mine_c] + [
-        lax.ppermute(mine_c, "col", [(s, (s + n) % ncol) for s in range(ncol)]) for n in range(1, ncol)
+        [lax.ppermute(mine_c[k], "col", [(s, (s + n) % ncol) for s in range(ncol)]) for k in range(PIV)]
+        for n in range(1, ncol)
     ]
 
     core = r % 2
@@ -155,11 +154,36 @@
             hop *= 2
         halves.append(part)
         others.append(lax.ppermute(part, "row", near))
-    half_own, half_other = jnp.stack(halves), jnp.stack(others)
-
-    parents = lax.all_gather(parent_of, "front", axis=0, tiled=True)
-    maps = lax.all_gather(child_map, "front", axis=0, tiled=True)
+
+    def corner(x, y):
+        orr, occ = order[x], order[y]
+        block = lax.dynamic_slice(matrix, (row_slot[x] * BS, col_slot[y] * BS), (BS, BS))
+        return jnp.where((orr // rb == r) & (occ // cb == c), block, 0.0)
+
+    def square(make, xs, ys):
+        return jnp.concatenate([jnp.concatenate([make(x, y) for y in ys], axis=1) for x in xs], axis=0)
+
+    pair = [square(corner, (0, 1), (2, 3)), square(corner, (2, 3), (0, 1))]
+    total = jnp.where(core == 0, pair[0], pair[1]) + lax.ppermute(
+        jnp.where(core == 0, pair[1], pair[0]), "row", near
+    )
+    hop = 2
+    while hop < nrow:
+        total = total + lax.ppermute(total, "row", [(s, s ^ hop) for s in range(nrow)])
+        hop *= 2
+    total = total + sum(
+        lax.ppermute(total, "col", [(s, (s + n) % ncol) for s in range(ncol)]) for n in range(1, ncol)
+    )
+
+    tables = lax.all_gather(jnp.concatenate([parent_of[:, None], child_map], axis=1), "front", axis=0, tiled=True)
+    parents, maps = tables[:, 0], tables[:, 1:]
     pieces = lax.all_gather(children, "front", axis=0, tiled=True)
+    early = PIV - 1
+    pieces, total, halves[:early], *firsts = lax.optimization_barrier(
+        (pieces, total, halves[:early], *[group[:early] for group in cands[1:]])
+    )
+    for group, first in zip(cands[1:], firsts):
+        group[:early] = first
     owned = jnp.argmax((parents == lax.axis_index("front")).astype(i32)).astype(i32)
     own_map = lax.dynamic_index_in_dim(maps, owned, 0, keepdims=False)
     piece = lax.dynamic_index_in_dim(pieces, owned, 0, keepdims=True)
@@ -191,17 +215,8 @@
     kinds = jnp.where(local_mask > 0, kinds, 0)
     kinds = jnp.where((pos_c < PIV) & (pos_r >= pos_c // 2 * 2 + 2), 4 + pos_c, kinds).astype(i32)
 
-    def corner(x, y):
-        orr, occ = order[x], order[y]
-        block = lax.dynamic_slice(matrix, (row_slot[x] * BS, col_slot[y] * BS), (BS, BS))
-        return jnp.where((orr // rb == r) & (occ // cb == c), block, 0.0)
-
-    def square(make, xs, ys):
-        return jnp.concatenate([jnp.concatenate([make(x, y) for y in ys], axis=1) for x in xs], axis=0)
-
-    corners = lax.psum(
-        jnp.stack([square(corner, (0, 1), (2, 3)), square(corner, (2, 3), (0, 1))]), ("row", "col")
-    )
+    partner = lax.ppermute(total, "row", near)
+    corners = (jnp.where(core == 0, total, partner), jnp.where(core == 0, partner, total))
     psrc, phas = picked(src), picked(has)
 
     def kid_corner(x, y):
@@ -241,7 +256,7 @@
         grid_spec=pltpu.PrefetchScalarGridSpec(
             num_scalar_prefetch=1,
             grid=(rb,),
-            in_specs=[pl.BlockSpec((BS, PIV * BS), lambda i, m: (i, 0))] * ncol
+            in_specs=[pl.BlockSpec((BS, BS), lambda i, m: (i, 0))] * (PIV * ncol)
             + [kid_spec(k) for k in range(PIV)]
             + [
                 pl.BlockSpec((1, 2, 2 * BS, 2 * BS), lambda i, m: (0, 0, 0, 0)),
@@ -252,14 +267,15 @@
         out_shape=[jax.ShapeDtypeStruct((loc_rows, PIV * BS), jnp.bfloat16)] * 2,
         compiler_params=params,
         name="lower",
-    )(meta, *cands, *[kid] * PIV, diag_inverse, u01)
+    )(meta, *[x for group in cands for x in group], *[kid] * PIV, diag_inverse, u01)
 
     n = max(cb, PIV)
     zero = jnp.zeros((n,), i32)
     held = (jnp.arange(cb, dtype=i32) // (cb // 2) == core).astype(i32)
     meta = jnp.stack(
         [pad(held, n), pad(cols_of(src), n), pad(cols_of(has), n), pad(psrc, n), pad(phas, n)]
-        + [zero] * 3
+        + [pad(jnp.clip(jnp.arange(cb, dtype=i32) - lead * (cb // 2), 0, cb // 2 - 1), n) for lead in (core, 1 - core)]
+        + [zero]
         + [pad(cols_of(mask_rows[k]), n) for k in range(PIV)]
     )
 
@@ -275,7 +291,8 @@
         grid_spec=pltpu.PrefetchScalarGridSpec(
             num_scalar_prefetch=1,
             grid=(cb,),
-            in_specs=[pl.BlockSpec((PIV, BS, BS), lambda j, m: (0, 0, j % (cb // 2)))] * 2
+            in_specs=[pl.BlockSpec((BS, BS), lambda j, m: (0, m[5, j]))] * PIV
+            + [pl.BlockSpec((BS, BS), lambda j, m: (0, m[6, j]))] * PIV
             + [kid_spec_up(k) for k in range(PIV)]
             + [pl.BlockSpec((2 * BS, 2 * BS), lambda j, m: (0, 0))],
             out_specs=[pl.BlockSpec((PIV * BS, BS), lambda j, m: (0, j))] * 2,
@@ -283,7 +300,7 @@
         out_shape=[jax.ShapeDtypeStruct((PIV * BS, loc_cols), jnp.bfloat16)] * 2,
         compiler_params=params,
         name="upper",
-    )(meta, half_own, half_other, *[kid] * PIV, l10)
+    )(meta, *halves, *others, *[kid] * PIV, l10)
 
     tile = min(4, cb)
     rows = jnp.stack([rows_of(has), rows_of(src)])

time: 613 us -> 490 us (0.80)
  the two profiles are of different devices: /device:TPU:0 before, /device:TPU:23 now
where the time goes in v2:
time: 490 us; the launch traced here: 481 us
  waiting for transfers between devices  237 us (48%)
  Pallas kernels  118 us (24%)
  between operations  46 us (9%)
  other arithmetic  34.4 us (7%)
  local copies, waits for them, and re-layouts  23.4 us (5%)
  starting transfers between devices  13.8 us (3%)
  blocking collectives  7.17 us (1%)
    ppermute x4, waiting for transfers between devices, body(): got = lax.ppermute(part, 'row', [(s, s ^ hop) for s in range(nrow)])  164 us
    pallas_call x1, Pallas kernels, body(): pl.pallas_call(functools.partial(trail_kernel, tile=tile, kc=kc), grid_sp...  76 us
    all_gather x1, waiting for transfers between devices, body(): kid = lax.all_gather(piece, ('row', 'col'), axis=0, tiled=True)  27.7 us
    pallas_call x1, Pallas kernels, body(): pl.pallas_call(upper_kernel, grid_spec=pltpu.PrefetchScalarGridSpec(num_s...  22.2 us
    ppermute x4, waiting for transfers between devices, body(): lax.ppermute(mine_c[k], 'col', [(s, (s + n) % ncol) for s in range(ncol)])  19.9 us
    pallas_call x1, Pallas kernels, body(): pl.pallas_call(functools.partial(lower_kernel, others=ncol - 1, cols=cb),...  19.6 us
    select_n x4, other arithmetic, body(): part = jnp.where(owner // hop % 2 == r // hop % 2, part, got)  13.1 us
    ppermute x1, waiting for transfers between devices, body(): lax.ppermute(total, 'row', [(s, s ^ hop) for s in range(nrow)])  10.2 us
  transfers between devices with their start and end apart: 22, of which 10 were waited for; matrix products, arithmetic and copies ran while one was open for 12% of the time, Pallas kernels for 4%

profile of v2, /device:TPU:23, one launch (start us, length us, event | category | flops | bytes accessed | tf_op | source)
XLA Modules:
  0.0 481.3 jit_solution(17924315023197240480)
XLA Ops:
  6.5 0.7 all-gather.4.cloned.1.call-update
  7.3 0.6 fusion.32
  15.4 7.9 %dynamic-slice_bitcast_fusion = (f32[256,2048]{1,0:T(8,128)}, f32[256,2048]{1,0:T(8,128)}, f32[256,2048]{1,0:T(8,128)}, f32[256,2048]{1,0:T(8,128)}) fusion(f32[1,2048,4096]{2,1,0:T(8,128)} %param.7, s32[]{:T(128)S(6)} %select_n.689, s32[]{:T(128)S(6)} %select_n.705, s32[]{:T(128)S(6)} %select_n.675, s32[]{:T(128)S(6)} %select_n.665, s32[]{:T(128)S(6)} %select_n.651), kind=kLoop, calls=%fused_computation.4 | loop fusion | bytes 16777236 | tf_op jit(solution)/shard_map/dynamic_slice | solution.py:146
  23.3 0.8 collective-permute-start.14
  24.2 0.5 collective-permute-start.5
  27.3 1.8 select_bitcast_fusion.15
  29.1 0.1 fusion.16
  29.3 0.6 collective-permute-start
  29.8 4.3 collective-permute-done
  34.1 1.5 select_add_fusion
  35.5 0.3 collective-permute-start.1
  35.9 2.9 collective-permute-done.3
  38.8 9.6 %bitcast_select_fusion = (f32[256,2048]{1,0:T(8,128)}, f32[256,2048]{1,0:T(8,128)}, f32[256,2048]{1,0:T(8,128)}, f32[256,2048]{1,0:T(8,128)}) fusion(f32[256,2048]{1,0:T(8,128)} %collective-permute-done.14, f32[1,2048,4096]{2,1,0:T(8,128)} %param.7, s32[]{:T(128)S(6)} %select_n.689, s32[]{:T(128)S(6)} %select_n.704, pred[]{:T(512)S(6)} %eq.316, ...), kind=kLoop, calls=%fused_computation | loop fusion | flops 2097152 | bytes 25165848 | tf_op jit(solution)/shard_map/jit(_where)/select_n | solution.py:149
  48.4 0.2 collective-permute-start.8
  48.7 1.2 collective-permute-start.6
  49.9 10.2 %collective-permute-done.1 = f32[512,512]{1,0:T(8,128)S(1)} collective-permute-done((f32[512,512]{1,0:T(8,128)S(1)}, f32[512,512]{1,0:T(8,128)S(1)}, u32[]{:S(2)}, u32[]{:S(2)}) %collective-permute-start.1) | collective-permute-done | bytes 1048608 | tf_op jit(solution)/shard_map/ppermute | solution.py:172
  60.1 0.2 add.352
  60.3 0.3 collective-permute-start.2
  60.6 0.2 collective-permute-start.4
  60.8 6.3 %dynamic-slice_bitcast_fusion.1 = (f32[2048,256]{1,0:T(8,128)S(1)}, f32[2048,256]{1,0:T(8,128)}, f32[2048,256]{1,0:T(8,128)}, f32[2048,256]{1,0:T(8,128)}) fusion(f32[1,2048,4096]{2,1,0:T(8,128)} %param.7, s32[]{:T(128)S(6)} %select_n.659, s32[]{:T(128)S(6)} %select_n.653, s32[]{:T(128)S(6)} %select_n.683, s32[]{:T(128)S(6)} %select_n.677), kind=kLoop, calls=%fused_computation.5 | loop fusion | bytes 16777232 | tf_op jit(solution)/shard_map/dynamic_slice | solution.py:133
  67.2 1.3 collective-permute-start.11
  69.2 7.2 %all-gather = s32[4,1,9]{2,1,0:T(1,128)S(1)} all-gather(s32[1,1,9]{2,1,0:T(1,128)S(1)} %add_bitcast_fusion), channel_id=1, replica_groups=mesh['front'=4,'row'=4,'col'=2] {'front'}, dimensions={0}, use_global_device_ids=true | all-gather | bytes 180 | tf_op jit(solution)/shard_map/all_gather | solution.py:178
  76.3 6.9 %collective-permute-done.2 = f32[512,512]{1,0:T(8,128)} collective-permute-done((f32[512,512]{1,0:T(8,128)S(1)}, f32[512,512]{1,0:T(8,128)}, u32[]{:S(2)}, u32[]{:S(2)}) %collective-permute-start.2) | collective-permute-done | bytes 1048608 | tf_op jit(solution)/shard_map/ppermute | solution.py:175
  83.3 0.2 collective-permute-start.10
  83.5 21.6 %collective-permute-done.8 = f32[256,2048]{1,0:T(8,128)} collective-permute-done((f32[256,2048]{1,0:T(8,128)}, f32[256,2048]{1,0:T(8,128)}, u32[]{:S(2)}, u32[]{:S(2)}) %collective-permute-start.8) | collective-permute-done | bytes 2097184 | tf_op jit(solution)/shard_map/ppermute | solution.py:152
  105.0 0.2 collective-permute-start.9
  105.2 0.1 convert_reduce_fusion.1
  105.4 0.7 iota_reduce_fusion
  108.3 1.8 add.353
  110.0 3.3 broadcast_select_fusion.1.refs_2_
  113.3 36.6 %collective-permute-done.6 = f32[256,2048]{1,0:T(8,128)} collective-permute-done((f32[256,2048]{1,0:T(8,128)}, f32[256,2048]{1,0:T(8,128)}, u32[]{:S(2)}, u32[]{:S(2)}) %collective-permute-start.6) | collective-permute-done | bytes 2097184 | tf_op jit(solution)/shard_map/ppermute | solution.py:152
  150.0 3.2 broadcast_select_fusion.2.refs_1_
  153.2 41.7 %collective-permute-done.4 = f32[256,2048]{1,0:T(8,128)} collective-permute-done((f32[256,2048]{1,0:T(8,128)}, f32[256,2048]{1,0:T(8,128)}, u32[]{:S(2)}, u32[]{:S(2)}) %collective-permute-start.4) | collective-permute-done | bytes 2097184 | tf_op jit(solution)/shard_map/ppermute | solution.py:152
  194.9 3.3 broadcast_select_fusion.3.refs_0_
  198.2 19.9 %collective-permute-done.9.refs_4_ = f32[2048,256]{1,0:T(8,128)} collective-permute-done((f32[2048,256]{1,0:T(8,128)}, f32[2048,256]{1,0:T(8,128)}, u32[]{:S(2)}, u32[]{:S(2)}) %collective-permute-start.9) | collective-permute-done | bytes 2097184 | tf_op jit(solution)/shard_map/ppermute | solution.py:135
  218.1 3.2 constant_dynamic-slice_fusion.8
  221.3 0.3 collective-permute-start.12
  221.6 0.1 fusion.19
  221.7 0.2 copy-done.3
  222.0 0.1 convert_reduce_fusion
  222.2 0.1 multiply_reduce_fusion
  222.3 0.2 select_reduce_fusion.2
  222.6 0.6 fusion.31
  232.8 0.6 fusion.30
  238.1 0.6 fusion.26
  239.9 0.6 fusion.27
  241.7 0.6 fusion.29
  243.5 0.7 fusion.28
  245.8 0.3 collective-permute-start.15
  246.9 3.1 collective-permute-start.13
  250.2 0.1 select_reduce_fusion
  250.4 0.5 collective-permute-start.17
  250.9 64.2 %collective-permute-done.15 = f32[256,2048]{1,0:T(8,128)} collective-permute-done((f32[256,2048]{1,0:T(8,128)}, f32[256,2048]{1,0:T(8,128)}, u32[]{:S(2)}, u32[]{:S(2)}) %collective-permute-start.15) | collective-permute-done | bytes 2097184 | tf_op jit(solution)/shard_map/ppermute | solution.py:152
  315.0 3.7 collective-permute-start.16
  318.8 3.3 broadcast_select_fusion.refs_3_
  322.2 0.1 select_select_fusion.kinds
  322.3 27.7 %all-gather.6.cloned.1.call-done = f32[8,512,1024]{2,1,0:T(8,128)} async-done(((f32[1,512,1024]{2,1,0:T(8,128)}), f32[8,512,1024]{2,1,0:T(8,128)}) %all-gather.6.cloned.1.call-update) | async-done | bytes 16777232 | tf_op jit(solution)/shard_map/all_gather | solution.py:190
  350.0 1.1 select_bitcast_fusion.7
  351.1 1.5 select_bitcast_fusion.3
  352.8 1.7 fusion.refs_13_
  354.4 19.6 %lower.1 = (bf16[2048,1024]{1,0:T(8,128)(2,1)}, bf16[2048,1024]{1,0:T(8,128)(2,1)}) custom-call(s32[12,8]{1,0:T(8,128)S(1)} %stack.83.meta, f32[2048,256]{1,0:T(8,128)} %get-tuple-element.54.refs_0_, f32[2048,256]{1,0:T(8,128)} %get-tuple-element.53.refs_1_, f32[2048,256]{1,0:T(8,128)} %get-tuple-element.52.refs_2_, f32[2048,256]{1,0:T(8,128)} %copy-done, ...), custom_call_target="tpu_custom_call" | custom-call | tf_op jit(solution)/shard_map/lower/pallas_call | solution.py:254
  374.2 2.0 fusion.2.refs_12_
  376.2 22.2 %upper.1 = (bf16[1024,4096]{1,0:T(8,128)(2,1)}, bf16[1024,4096]{1,0:T(8,128)(2,1)}) custom-call(s32[12,16]{1,0:T(8,128)S(1)} %stack.86.meta, f32[256,2048]{1,0:T(8,128)} %broadcast_select_fusion.3.refs_0_, f32[256,2048]{1,0:T(8,128)} %broadcast_select_fusion.2.refs_1_, f32[256,2048]{1,0:T(8,128)} %broadcast_select_fusion.1.refs_2_, ...), custom_call_target="tpu_custom_call" | custom-call | tf_op jit(solution)/shard_map/upper/pallas_call | solution.py:289
  398.4 76.0 %trail.1 = f32[2048,4096]{1,0:T(8,128)} custom-call(s32[2,8]{1,0:T(2,128)S(1)} %pad_add_fusion.rows, s32[2,16]{1,0:T(2,128)S(1)} %pad_add_fusion.1.cols, s32[8,16]{1,0:T(8,128)S(1)} %select_select_fusion.kinds, f32[2048,4096]{1,0:T(8,128)} %bitcast.140, f32[4,2,512,1024]{3,2,1,0:T(8,128)} %bitcast.139, bf16[2048,1024]{1,0:T(8,128)(2,1)} %get-tuple-element.24.lh, ...), custom_call_target="tpu_custom_call" | custom-call | tf_op jit(solution)/shard_map/trail/pallas_call | solution.py:308
  (84 shorter events, 2.0 us)
Async XLA Ops:
  6.5 0.8 copy-start.4
  6.5 211.5 %all-gather.4.cloned.1.call-start = ((), (), s32[]{:S(2)}) async-start(), calls=%async_computation | async-start | bytes 10485760 | tf_op jit(solution)/shard_map/all_gather | solution.py:180
  7.3 342.8 %all-gather.6.cloned.1.call-start = ((), (), s32[]{:S(2)}) async-start(), calls=%async_computation.1 | async-start | bytes 18874368 | tf_op jit(solution)/shard_map/all_gather | solution.py:190
  23.3 12.5 %collective-permute-start.14 = (f32[256,2048]{1,0:T(8,128)}, f32[256,2048]{1,0:T(8,128)}, u32[]{:S(2)}, u32[]{:S(2)}) collective-permute-start(f32[256,2048]{1,0:T(8,128)} %get-tuple-element.47), channel_id=1, source_target_pairs={{0,2},{2,0},{4,6},{6,4},{1,3},{3,1},{5,7},{7,5},{8,10},{10,8},{12,... | collective-permute-start | bytes 6291464 | tf_op jit(solution)/shard_map/ppermute | solution.py:148
  24.2 11.7 %collective-permute-start.7 = (f32[256,2048]{1,0:T(8,128)}, f32[256,2048]{1,0:T(8,128)}, u32[]{:S(2)}, u32[]{:S(2)}) collective-permute-start(f32[256,2048]{1,0:T(8,128)} %get-tuple-element.48), channel_id=1, source_target_pairs={{0,2},{2,0},{4,6},{6,4},{1,3},{3,1},{5,7},{7,5},{8,10},{10,8},{12,... | collective-permute-start | bytes 6291464 | tf_op jit(solution)/shard_map/ppermute | solution.py:148
  24.2 11.7 %collective-permute-start.5 = (f32[256,2048]{1,0:T(8,128)}, f32[256,2048]{1,0:T(8,128)}, u32[]{:S(2)}, u32[]{:S(2)}) collective-permute-start(f32[256,2048]{1,0:T(8,128)} %get-tuple-element.49), channel_id=1, source_target_pairs={{0,2},{2,0},{4,6},{6,4},{1,3},{3,1},{5,7},{7,5},{8,10},{10,8},{12,... | collective-permute-start | bytes 6291464 | tf_op jit(solution)/shard_map/ppermute | solution.py:148
  24.7 14.1 %collective-permute-start.3 = (f32[256,2048]{1,0:T(8,128)}, f32[256,2048]{1,0:T(8,128)}, u32[]{:S(2)}, u32[]{:S(2)}) collective-permute-start(f32[256,2048]{1,0:T(8,128)} %get-tuple-element.50), channel_id=1, source_target_pairs={{0,2},{2,0},{4,6},{6,4},{1,3},{3,1},{5,7},{7,5},{8,10},{10,8},{12,... | collective-permute-start | bytes 6291464 | tf_op jit(solution)/shard_map/ppermute | solution.py:148
  29.3 4.8 %collective-permute-start = (f32[512,512]{1,0:T(8,128)S(1)}, f32[512,512]{1,0:T(8,128)}, u32[]{:S(2)}, u32[]{:S(2)}) collective-permute-start(f32[512,512]{1,0:T(8,128)S(1)} %fusion.16), channel_id=1, source_target_pairs={{0,2},{2,0},{4,6},{6,4},{1,3},{3,1},{5,7},{7,5},{8,10},{10,8},{12,... | collective-permute-start | bytes 3145736 | tf_op jit(solution)/shard_map/ppermute | solution.py:167
  35.5 24.5 %collective-permute-start.1 = (f32[512,512]{1,0:T(8,128)S(1)}, f32[512,512]{1,0:T(8,128)S(1)}, u32[]{:S(2)}, u32[]{:S(2)}) collective-permute-start(f32[512,512]{1,0:T(8,128)S(1)} %select_add_fusion), channel_id=1, source_target_pairs={{0,4},{2,6},{4,0},{6,2},{1,5},{3,7},{5,1},{7,3},{8,12},{10,14},{12... | collective-permute-start | bytes 3145736 | tf_op jit(solution)/shard_map/ppermute | solution.py:172
  48.4 56.6 %collective-permute-start.8 = (f32[256,2048]{1,0:T(8,128)}, f32[256,2048]{1,0:T(8,128)}, u32[]{:S(2)}, u32[]{:S(2)}) collective-permute-start(f32[256,2048]{1,0:T(8,128)} %get-tuple-element.44), channel_id=1, source_target_pairs={{0,4},{2,6},{4,0},{6,2},{1,5},{3,7},{5,1},{7,3},{8,12},{10,14},{12... | collective-permute-start | bytes 6291464 | tf_op jit(solution)/shard_map/ppermute | solution.py:152
  48.7 101.3 %collective-permute-start.6 = (f32[256,2048]{1,0:T(8,128)}, f32[256,2048]{1,0:T(8,128)}, u32[]{:S(2)}, u32[]{:S(2)}) collective-permute-start(f32[256,2048]{1,0:T(8,128)} %get-tuple-element.45), channel_id=1, source_target_pairs={{0,4},{2,6},{4,0},{6,2},{1,5},{3,7},{5,1},{7,3},{8,12},{10,14},{12... | collective-permute-start | bytes 6291464 | tf_op jit(solution)/shard_map/ppermute | solution.py:152
  60.3 6.9 %copy-start.2 = (f32[512,512]{1,0:T(8,128)}, f32[512,512]{1,0:T(8,128)S(1)}, u32[]{:S(2)}) copy-start(f32[512,512]{1,0:T(8,128)S(1)} %add.352) | copy-start | bytes 3145732
  60.3 22.9 %collective-permute-start.2 = (f32[512,512]{1,0:T(8,128)S(1)}, f32[512,512]{1,0:T(8,128)}, u32[]{:S(2)}, u32[]{:S(2)}) collective-permute-start(f32[512,512]{1,0:T(8,128)S(1)} %add.352), channel_id=1, source_target_pairs={{0,1},{1,0},{2,3},{3,2},{4,5},{5,4},{6,7},{7,6},{8,9},{9,8},{10,11... | collective-permute-start | bytes 3145736 | tf_op jit(solution)/shard_map/ppermute | solution.py:175
  60.6 8.5 %copy-start.5 = (s32[1,8]{1,0:T(1,128)S(1)}, s32[1,8]{1,0:T(1,128)}, u32[]{:S(2)}) copy-start(s32[1,8]{1,0:T(1,128)} %param.10) | copy-start | bytes 100
  60.6 134.3 %collective-permute-start.4 = (f32[256,2048]{1,0:T(8,128)}, f32[256,2048]{1,0:T(8,128)}, u32[]{:S(2)}, u32[]{:S(2)}) collective-permute-start(f32[256,2048]{1,0:T(8,128)} %get-tuple-element.46), channel_id=1, source_target_pairs={{0,4},{2,6},{4,0},{6,2},{1,5},{3,7},{5,1},{7,3},{8,12},{10,14},{12... | collective-permute-start | bytes 6291464 | tf_op jit(solution)/shard_map/ppermute | solution.py:152
  67.2 154.1 %copy-start = (f32[2048,256]{1,0:T(8,128)}, f32[2048,256]{1,0:T(8,128)S(1)}, u32[]{:S(2)}) copy-start(f32[2048,256]{1,0:T(8,128)S(1)} %get-tuple-element.51.refs_3_) | copy-start | bytes 6291460
  67.2 131.0 %collective-permute-start.11 = (f32[2048,256]{1,0:T(8,128)}, f32[2048,256]{1,0:T(8,128)}, u32[]{:S(2)}, u32[]{:S(2)}) collective-permute-start(f32[2048,256]{1,0:T(8,128)} %get-tuple-element.52.refs_2_), channel_id=1, source_target_pairs={{0,1},{1,0},{2,3},{3,2},{4,5},{5,4},{6,7},{7,6},{8,9},{9,8},{10,11... | collective-permute-start | bytes 6291464 | tf_op jit(solution)/shard_map/ppermute | solution.py:135
  83.3 115.0 %collective-permute-start.10 = (f32[2048,256]{1,0:T(8,128)}, f32[2048,256]{1,0:T(8,128)}, u32[]{:S(2)}, u32[]{:S(2)}) collective-permute-start(f32[2048,256]{1,0:T(8,128)} %get-tuple-element.53.refs_1_), channel_id=1, source_target_pairs={{0,1},{1,0},{2,3},{3,2},{4,5},{5,4},{6,7},{7,6},{8,9},{9,8},{10,11... | collective-permute-start | bytes 6291464 | tf_op jit(solution)/shard_map/ppermute | solution.py:135
  105.0 113.0 %collective-permute-start.9 = (f32[2048,256]{1,0:T(8,128)}, f32[2048,256]{1,0:T(8,128)}, u32[]{:S(2)}, u32[]{:S(2)}) collective-permute-start(f32[2048,256]{1,0:T(8,128)} %get-tuple-element.54.refs_0_), channel_id=1, source_target_pairs={{0,1},{1,0},{2,3},{3,2},{4,5},{5,4},{6,7},{7,6},{8,9},{9,8},{10,11... | collective-permute-start | bytes 6291464 | tf_op jit(solution)/shard_map/ppermute | solution.py:135
  221.2 0.7 copy-start.3
  221.3 133.2 %collective-permute-start.12 = (f32[2048,256]{1,0:T(8,128)S(1)}, f32[2048,256]{1,0:T(8,128)}, u32[]{:S(2)}, u32[]{:S(2)}) collective-permute-start(f32[2048,256]{1,0:T(8,128)S(1)} %get-tuple-element.51.refs_3_), channel_id=1, source_target_pairs={{0,1},{1,0},{2,3},{3,2},{4,5},{5,4},{6,7},{7,6},{8,9},{9,8},{10,11... | collective-permute-start | bytes 6291464 | tf_op jit(solution)/shard_map/ppermute | solution.py:135
  245.8 69.2 %collective-permute-start.15 = (f32[256,2048]{1,0:T(8,128)}, f32[256,2048]{1,0:T(8,128)}, u32[]{:S(2)}, u32[]{:S(2)}) collective-permute-start(f32[256,2048]{1,0:T(8,128)} %get-tuple-element.43), channel_id=1, source_target_pairs={{0,4},{2,6},{4,0},{6,2},{1,5},{3,7},{5,1},{7,3},{8,12},{10,14},{12... | collective-permute-start | bytes 6291464 | tf_op jit(solution)/shard_map/ppermute | solution.py:152
  246.9 75.2 %collective-permute-start.13 = (f32[512,512]{1,0:T(8,128)S(1)}, f32[512,512]{1,0:T(8,128)}, u32[]{:S(2)}, u32[]{:S(2)}) collective-permute-start(f32[512,512]{1,0:T(8,128)S(1)} %add.353), channel_id=1, source_target_pairs={{0,2},{2,0},{4,6},{6,4},{1,3},{3,1},{5,7},{7,5},{8,10},{10,8},{12,... | collective-permute-start | bytes 3145736 | tf_op jit(solution)/shard_map/ppermute | solution.py:218
  250.4 125.8 %collective-permute-start.18 = (f32[256,2048]{1,0:T(8,128)}, f32[256,2048]{1,0:T(8,128)}, u32[]{:S(2)}, u32[]{:S(2)}) collective-permute-start(f32[256,2048]{1,0:T(8,128)} %broadcast_select_fusion.1.refs_2_), channel_id=1, source_target_pairs={{0,2},{2,0},{4,6},{6,4},{1,3},{3,1},{5,7},{7,5},{8,10},{10,8},{12,... | collective-permute-start | bytes 6291464 | tf_op jit(solution)/shard_map/ppermute | solution.py:156
  250.4 125.8 %collective-permute-start.17 = (f32[256,2048]{1,0:T(8,128)}, f32[256,2048]{1,0:T(8,128)}, u32[]{:S(2)}, u32[]{:S(2)}) collective-permute-start(f32[256,2048]{1,0:T(8,128)} %broadcast_select_fusion.2.refs_1_), channel_id=1, source_target_pairs={{0,2},{2,0},{4,6},{6,4},{1,3},{3,1},{5,7},{7,5},{8,10},{10,8},{12,... | collective-permute-start | bytes 6291464 | tf_op jit(solution)/shard_map/ppermute | solution.py:156
  315.0 61.1 %collective-permute-start.16 = (f32[256,2048]{1,0:T(8,128)}, f32[256,2048]{1,0:T(8,128)}, u32[]{:S(2)}, u32[]{:S(2)}) collective-permute-start(f32[256,2048]{1,0:T(8,128)} %broadcast_select_fusion.3.refs_0_), channel_id=1, source_target_pairs={{0,2},{2,0},{4,6},{6,4},{1,3},{3,1},{5,7},{7,5},{8,10},{10,8},{12,... | collective-permute-start | bytes 6291464 | tf_op jit(solution)/shard_map/ppermute | solution.py:156
  322.0 54.1 %collective-permute-start.19 = (f32[256,2048]{1,0:T(8,128)}, f32[256,2048]{1,0:T(8,128)}, u32[]{:S(2)}, u32[]{:S(2)}) collective-permute-start(f32[256,2048]{1,0:T(8,128)} %broadcast_select_fusion.refs_3_), channel_id=1, source_target_pairs={{0,2},{2,0},{4,6},{6,4},{1,3},{3,1},{5,7},{7,5},{8,10},{10,8},{12,... | collective-permute-start | bytes 6291464 | tf_op jit(solution)/shard_map/ppermute | solution.py:156
  354.4 19.7 %copy-start.1 = (f32[1,2,512,512]{3,2,1,0:T(8,128)S(1)}, f32[1,2,512,512]{3,2,1,0:T(8,128)}, u32[]{:S(2)}) copy-start(f32[1,2,512,512]{3,2,1,0:T(8,128)} %refs_12_.1) | copy-start | bytes 6291460
Sparse Core Ops, SparseCore 0:
  8.9 148.8 all-gather.3
  221.4 128.5 all-gather.5
